TPU v7x, 768 devices: a whole 4x8x12 slice. The times are simulated.
768 devices in a mesh: row: 48 (over x, z), split: 16 (over y, core).
Axes of the slice: x: 4, y: 8, z: 12, core: 2. Of those that a mesh axis runs over, the one named last changes fastest.
Arguments:
- tiles: bfloat16 [73728, 4096], P(('row', 'split')), may hold values from -6 to 6
- tile_dest: int32 [73728, 1], P(('row', 'split')), may hold values from 0 to 47; in each aligned block of 96 rows (0 to 95, 96 to 191, ...) at most 3 rows name the same one
- tile_row: int32 [73728], P(('row', 'split')), may hold values from 0 to 31
- tile_col: int32 [73728], P(('row', 'split')), may hold values from 0 to 15
- density: bfloat16 [16384, 256], P('split'), may hold values from -0.109375 to 0.109375
Outputs:
- contracted: bfloat16 [98304, 256], P(('row', 'split'))
Inputs may be any that keep to these rules, and one draw needn't show every extreme that they name: `tile_dest`: within the blocks of one device (aligned runs of 96 blocks) no row owner is named more than 3 times.
All inputs are finite; a program needn't handle non-finite values.
Results may differ from a plain program's by a relative error of at most 0.001.
Values may be sent and summed in bfloat16 or wider, within the bound.
A program may use at most 32 MiB of HBM per device.

v0:
```python
import jax
import jax.numpy as jnp
from jax import lax
from jax.sharding import PartitionSpec as P

B = 64
RBLK = 32


def on_device(tiles, tile_dest, tile_row, tile_col, density):
    owners = lax.axis_size("row")
    count = tiles.shape[0]
    flat = tiles.shape[1]
    width = B
    orbitals = density.shape[1]
    nublocks = density.shape[0] // width
    capacity = (5 * count + 4 * owners - 1) // (4 * owners)
    total_rows = RBLK * width
    target = tile_dest[:, 0]
    onehot = (target[:, None] == jnp.arange(owners, dtype=jnp.int32)[None, :]).astype(jnp.int32)
    earlier = jnp.cumsum(onehot, axis=0) - onehot
    slot = jnp.sum(earlier * onehot, axis=1)
    send_tiles = jnp.zeros((owners, capacity, flat), jnp.bfloat16).at[target, slot].set(tiles)
    labels = jnp.stack([tile_row, tile_col], axis=1)
    send_labels = jnp.full((owners, capacity, 2), -1, jnp.int32).at[target, slot].set(labels)
    recv_tiles, recv_labels = (
        lax.all_to_all(send_tiles, "row", split_axis=0, concat_axis=0, tiled=True),
        lax.all_to_all(send_labels, "row", split_axis=0, concat_axis=0, tiled=True),
    )
    dens_blocks = density.reshape(nublocks, width, orbitals)
    offsets = jnp.arange(width, dtype=jnp.int32)

    def add_group(part, group_tiles, group_rows, group_cols, keep, span):
        group_tiles = group_tiles.reshape(-1, width, width)
        picked = dens_blocks[jnp.clip(group_cols, 0, nublocks - 1)]
        product = jnp.einsum(
            "sab,sbo->sao", group_tiles, picked, preferred_element_type=jnp.float32
        )
        place = group_rows[:, None] * width + offsets[None, :]
        inside = keep[:, None] & (group_rows[:, None] >= 0) & (place >= 0) & (place < span)
        place = jnp.where(inside, place, span)
        return part.at[place.reshape(-1)].add(product.reshape(-1, orbitals), mode="drop")

    def turn(slot_index, part):
        tile_slot = lax.dynamic_index_in_dim(recv_tiles, slot_index, 1, keepdims=False)
        label_slot = lax.dynamic_index_in_dim(recv_labels, slot_index, 1, keepdims=False)
        keep = jnp.ones((owners,), jnp.bool_)
        return add_group(part, tile_slot, label_slot[:, 0], label_slot[:, 1], keep, total_rows)

    partial_rows = lax.fori_loop(0, capacity, turn, jnp.zeros((total_rows, orbitals), jnp.float32))
    summed = lax.psum_scatter(partial_rows, "split", scatter_dimension=0, tiled=True)
    return summed.astype(jnp.bfloat16)


def solution(mesh):
    placed = (
        P(("row", "split"), None),
        P(("row", "split"), None),
        P(("row", "split")),
        P(("row", "split")),
        P("split", None),
    )
    return jax.shard_map(
        on_device, mesh=mesh, in_specs=placed, out_specs=P(("row", "split"), None), check_vma=False
    )
```

profile of v0, /device:TPU:1, one launch (start us, length us, event | category | flops | bytes accessed | tf_op | source)
XLA Modules:
  0.0 276.0 jit_solution(5852075470854250098)
XLA Ops:
  6.5 0.0 copy-start.2
  6.5 0.8 fusion.3
  7.3 0.1 reduce_window_sum.11
  7.5 0.8 select_reduce_fusion
  8.3 0.7 fusion.5
  9.0 0.7 pad_add_fusion
  9.7 0.1 copy.8
  9.8 5.4 %scatter_fusion.1 = s32[48,3,2]{2,0,1:T(8,128)S(1)} fusion(s32[48,3,2]{2,0,1:T(8,128)S(1)} %broadcast_in_dim.26, s32[96]{0:T(128)S(1)} %fusion.5, s32[96,2]{1,0:T(8,128)S(1)} %copy.8), kind=kCustom, calls=%fused_computation.2 | custom fusion | bytes 3072 | tf_op jit(solution)/shard_map/scatter | solution.py:25
  15.2 1.0 copy.9
  16.2 18.8 %all-to-all-start = ((s32[48,3,2]{1,2,0:T(2,128)}), s32[48,3,2]{1,2,0:T(2,128)S(1)}, u32[]{:S(2)}, u32[]{:S(2)}) async-start(s32[48,3,2]{1,2,0:T(2,128)} %copy.9), calls=%async_computation | async-start | bytes 98304 | tf_op jit(solution)/shard_map/all_to_all | solution.py:28
  35.0 0.1 broadcast_in_dim.27
  35.2 0.0 copy-done.2
  35.2 14.5 %scatter_fusion.2 = bf16[48,3,4096]{2,0,1:T(8,128)(2,1)S(1)} fusion(bf16[48,3,4096]{2,0,1:T(8,128)(2,1)S(1)} %broadcast_in_dim.27, s32[96]{0:T(128)S(1)} %fusion.5, bf16[96,4096]{1,0:T(8,128)(2,1)S(1)} %copy-done.2), kind=kCustom, calls=%fused_computation.3 | custom fusion | bytes 2360064 | tf_op jit(solution)/shard_map/scatter | solution.py:23
  49.7 2.2 copy.10
  51.9 0.0 all-to-all-done
  51.9 11.9 %all-to-all-start.1 = ((bf16[48,3,4096]{2,1,0:T(4,128)(2,1)}), bf16[48,3,4096]{2,1,0:T(4,128)(2,1)S(1)}, u32[]{:S(2)}, u32[]{:S(2)}) async-start(bf16[48,3,4096]{2,1,0:T(4,128)(2,1)} %copy.10), calls=%async_computation.1 | async-start | bytes 3145728 | tf_op jit(solution)/shard_map/all_to_all | solution.py:27
  63.8 0.0 reduce-scatter.2.cloned.1.call-start
  63.9 0.1 copy.11
  64.0 52.3 %all-to-all-done.1 = bf16[48,3,4096]{2,1,0:T(4,128)(2,1)S(1)} async-done(((bf16[48,3,4096]{2,1,0:T(4,128)(2,1)}), bf16[48,3,4096]{2,1,0:T(4,128)(2,1)S(1)}, u32[]{:S(2)}, u32[]{:S(2)}) %all-to-all-start.1) | async-done | bytes 1179680 | tf_op jit(solution)/shard_map/all_to_all | solution.py:27
  116.3 1.9 copy.12
  118.2 0.0 copy-start.1
  118.2 0.1 broadcast_in_dim.25
  118.3 0.9 copy-done.1
  119.2 82.9 %while.14 = (s32[]{:T(128)}, f32[2048,256]{1,0:T(8,128)S(1)}, s32[48,3,2]{0,2,1:T(2,128)S(1)}, bf16[48,3,4096]{2,0,1:T(8,128)(2,1)}, bf16[16,64,256]{2,1,0:T(8,128)(2,1)S(1)}, /*index=5*/s32[]{:T(128)}) while((s32[]{:T(128)}, f32[2048,256]{1,0:T(8,128)S(1)}, s32[48,3,2]{0,2,1:T(2,128)S(1)}, bf16[48,3,4096]{2,0,1:T(8,128)(2,1)}, ...), condition=%wide.region_6.7_spmd.clone, body=%wide.region_4.6_spmd.clone.sunk | while | flops 101478688 | bytes 19360172 | solution.py:50
  119.2 1.9 gather_fusion
  121.1 1.8 constant_dynamic-slice_fusion.2
  122.8 1.8 reshape.139
  124.6 3.6 %fusion.16 = f32[48,64,256]{2,1,0:T(8,128)} fusion(bf16[48,64,64]{2,1,0:T(8,128)(2,1)S(1)} %reshape.139, bf16[48,64,256]{2,1,0:T(8,128)(2,1)} %gather_fusion), kind=kOutput, calls=%fused_computation.26.clone.1 | convolution fusion | flops 100663296 | bytes 5111808 | tf_op jit(solution)/shard_map/while/body/eval_jaxpr/sab,sbo->sao/dot_general | solution.py:36
  128.2 0.1 iota_add_fusion.2
  128.3 0.1 add.149
  128.4 0.1 and.72
  128.5 0.1 and.73
  128.6 18.2 %scatter_fusion = f32[2048,256]{1,0:T(8,128)S(1)} fusion(f32[2048,256]{1,0:T(8,128)S(1)} %get-tuple-element.191, s32[3072]{0:T(1024)S(1)} %bitcast.40, f32[3072,256]{1,0:T(8,128)} %bitcast.38), kind=kCustom, calls=%fused_computation.1.clone.clone.1 | custom fusion | flops 786432 | bytes 9449472 | tf_op jit(solution)/shard_map/while/body/eval_jaxpr/scatter-add | solution.py:42
  146.9 1.9 gather_fusion
  148.7 1.8 constant_dynamic-slice_fusion.2
  150.5 1.8 reshape.139
  152.3 3.6 %fusion.16 = f32[48,64,256]{2,1,0:T(8,128)} fusion(bf16[48,64,64]{2,1,0:T(8,128)(2,1)S(1)} %reshape.139, bf16[48,64,256]{2,1,0:T(8,128)(2,1)} %gather_fusion), kind=kOutput, calls=%fused_computation.26.clone.1 | convolution fusion | flops 100663296 | bytes 5111808 | tf_op jit(solution)/shard_map/while/body/eval_jaxpr/sab,sbo->sao/dot_general | solution.py:36
  155.9 0.1 iota_add_fusion.2
  156.0 0.1 add.149
  156.1 0.1 and.72
  156.1 0.1 and.73
  156.3 18.2 %scatter_fusion = f32[2048,256]{1,0:T(8,128)S(1)} fusion(f32[2048,256]{1,0:T(8,128)S(1)} %get-tuple-element.191, s32[3072]{0:T(1024)S(1)} %bitcast.40, f32[3072,256]{1,0:T(8,128)} %bitcast.38), kind=kCustom, calls=%fused_computation.1.clone.clone.1 | custom fusion | flops 786432 | bytes 9449472 | tf_op jit(solution)/shard_map/while/body/eval_jaxpr/scatter-add | solution.py:42
  174.5 1.9 gather_fusion
  176.4 1.8 constant_dynamic-slice_fusion.2
  178.1 1.8 reshape.139
  179.9 3.6 %fusion.16 = f32[48,64,256]{2,1,0:T(8,128)} fusion(bf16[48,64,64]{2,1,0:T(8,128)(2,1)S(1)} %reshape.139, bf16[48,64,256]{2,1,0:T(8,128)(2,1)} %gather_fusion), kind=kOutput, calls=%fused_computation.26.clone.1 | convolution fusion | flops 100663296 | bytes 5111808 | tf_op jit(solution)/shard_map/while/body/eval_jaxpr/sab,sbo->sao/dot_general | solution.py:36
  183.5 0.1 iota_add_fusion.2
  183.6 0.1 add.149
  183.7 0.1 and.72
  183.8 0.1 and.73
  183.9 18.2 %scatter_fusion = f32[2048,256]{1,0:T(8,128)S(1)} fusion(f32[2048,256]{1,0:T(8,128)S(1)} %get-tuple-element.191, s32[3072]{0:T(1024)S(1)} %bitcast.40, f32[3072,256]{1,0:T(8,128)} %bitcast.38), kind=kCustom, calls=%fused_computation.1.clone.clone.1 | custom fusion | flops 786432 | bytes 9449472 | tf_op jit(solution)/shard_map/while/body/eval_jaxpr/scatter-add | solution.py:42
  202.1 0.0 copy-start
  202.1 1.3 copy-done
  203.5 0.0 reduce-scatter.2.cloned.1.call-update
  203.5 64.1 %reduce-scatter.2.cloned.1.call-done = f32[128,256]{1,0:T(8,128)} async-done(((f32[2048,256]{1,0:T(8,128)}), f32[128,256]{1,0:T(8,128)}) %reduce-scatter.2.cloned.1.call-update) | async-done | bytes 131088 | tf_op jit(solution)/shard_map/reduce_scatter | solution.py:51
  267.6 1.5 convert_element_type.7
  (16 shorter events, 0.2 us)
Async XLA Ops:
  6.5 28.6 %copy-start.2 = (bf16[96,4096]{1,0:T(8,128)(2,1)S(1)}, bf16[96,4096]{1,0:T(8,128)(2,1)}, u32[]{:S(2)}) copy-start(bf16[96,4096]{1,0:T(8,128)(2,1)} %param.7) | copy-start | bytes 2359300
  16.2 35.7 %all-to-all-start = ((s32[48,3,2]{1,2,0:T(2,128)}), s32[48,3,2]{1,2,0:T(2,128)S(1)}, u32[]{:S(2)}, u32[]{:S(2)}) async-start(s32[48,3,2]{1,2,0:T(2,128)} %copy.9), calls=%async_computation | async-start | bytes 98304 | tf_op jit(solution)/shard_map/all_to_all | solution.py:28
  51.9 64.4 %all-to-all-start.1 = ((bf16[48,3,4096]{2,1,0:T(4,128)(2,1)}), bf16[48,3,4096]{2,1,0:T(4,128)(2,1)S(1)}, u32[]{:S(2)}, u32[]{:S(2)}) async-start(bf16[48,3,4096]{2,1,0:T(4,128)(2,1)} %copy.10), calls=%async_computation.1 | async-start | bytes 3145728 | tf_op jit(solution)/shard_map/all_to_all | solution.py:27
  63.8 203.8 %reduce-scatter.2.cloned.1.call-start = ((), (), s32[]{:S(2)}) async-start(), calls=%async_computation.3 | async-start | bytes 2228224 | tf_op jit(solution)/shard_map/reduce_scatter | solution.py:51
  118.2 1.0 copy-start.1
  202.1 1.4 copy-start
Sparse Core Ops, SparseCore 0:
  203.6 63.9 reduce-scatter.1
where the time goes:
time: 277 us; the launch traced here: 276 us
  waiting for transfers between devices  116 us (42%)
  other arithmetic  59.6 us (22%)
  local copies, waits for them, and re-layouts  44.6 us (16%)
  starting transfers between devices  30.8 us (11%)
  between operations  13.5 us (5%)
  matrix products  10.9 us (4%)
    reduce_scatter x1, waiting for transfers between devices, on_device(): lax.psum_scatter(partial_rows, 'split', scatter_dimension=0, tiled=True)  64.1 us
    scatter-add x3, other arithmetic, add_group(): part.at[place.reshape(-1)].add(product.reshape(-1, orbitals), mode='drop')  54.6 us
    all_to_all x1, waiting for transfers between devices, on_device(): lax.all_to_all(send_tiles, 'row', split_axis=0, concat_axis=0, tiled=True)  52.3 us
    all_to_all x1, starting transfers between devices, on_device(): lax.all_to_all(send_labels, 'row', split_axis=0, concat_axis=0, tiled=True)  18.8 us
    scatter x2, local copies, waits for them, and re-layouts, on_device(): jnp.zeros((owners, capacity, flat), jnp.bfloat16).at[target, slot]  16.7 us
    all_to_all x1, starting transfers between devices, on_device(): lax.all_to_all(send_tiles, 'row', split_axis=0, concat_axis=0, tiled=True)  11.9 us
    dot_general x3, matrix products, add_group(): jnp.einsum('sab,sbo->sao', group_tiles, picked, preferred_element_type=jn...  10.9 us
    scatter x2, local copies, waits for them, and re-layouts, on_device(): jnp.full((owners, capacity, 2), -1, jnp.int32).at[target, slot].set(labels)  6.39 us
  transfers between devices with their start and end apart: 3, of which 2 were waited for; matrix products, arithmetic and copies ran while one was open for 6% of the time, Pallas kernels for 0%

commit v1 on v0

v1 whole, which is shorter than its diff:
```python
import functools

import jax
import jax.numpy as jnp
from jax import lax
from jax.experimental import pallas as pl
from jax.experimental.pallas import tpu as pltpu
from jax.sharding import PartitionSpec as P

MESH = pl.DeviceIdType.MESH
B = 64
LANES = 128
ROWS = B * B // LANES
CAP = 3
NX = 4


def shift(at, by, size):
    return lax.rem(at + by, size)


def kernel(
    n_row, n_split, meta_ref, tiles_ref, dens_ref, out_ref,
    pack, pack_s, send, recv, lab_send, lab_recv, plan, plan_s, sums,
    xsend, xrecv, usend, urecv, dsend, drecv,
    local_sem, lab_ss, lab_rs, tile_ss, tile_rs, x_ss, x_rs, u_ss, u_rs, d_ss, d_rs,
):
    nz, ny = n_row // NX, n_split // 2
    count = tiles_ref.shape[0]
    half = ny // 2
    slots = n_row * CAP
    row, split = lax.axis_index("row"), lax.axis_index("split")
    x, z = row // nz, lax.rem(row, nz)
    y, core = split // 2, lax.rem(split, 2)
    other = (row, y * 2 + 1 - core)
    above = (row, shift(y, 1, ny) * 2 + core)
    below = (row, shift(y, ny - 1, ny) * 2 + core)

    def offset(q):
        u = (n_row - q) % n_row
        k = u // NX
        odd = k % 2
        return u % NX, odd * ((k + 1) // 2) + (1 - odd) * ((nz - k // 2) % nz)

    def owner(q):
        dx, dz = offset(q)
        return (x + dx) % NX * nz + (z + dz) % nz

    barrier = pltpu.get_barrier_semaphore()

    def greet(q, carry):
        pl.semaphore_signal(barrier, inc=1, device_id=(owner(q), split), device_id_type=MESH)
        return carry

    lax.fori_loop(1, n_row, greet, 0)
    for peer in (other, above, below):
        pl.semaphore_signal(barrier, inc=1, device_id=peer, device_id_type=MESH)

    dest = meta_ref[0:1, :]
    label = meta_ref[1:2, :]
    width = dest.shape[1]
    t_sub = lax.broadcasted_iota(jnp.int32, (width, width), 0)
    t_lane = lax.broadcasted_iota(jnp.int32, (width, width), 1)
    dest_col = jnp.sum(jnp.where(t_sub == t_lane, dest, 0), axis=1, keepdims=True)
    rank = jnp.sum(jnp.where((dest_col == dest) & (t_sub < t_lane), 1, 0), axis=0, keepdims=True)
    q_sub = lax.broadcasted_iota(jnp.int32, (n_row, LANES), 0)
    lane = lax.broadcasted_iota(jnp.int32, (n_row, LANES), 1)
    u = jnp.where(q_sub == 0, 0, n_row - q_sub)
    k = u // NX
    dz = jnp.where(k % 2 == 1, (k + 1) // 2, (nz - k // 2) % nz)
    to = (x + u % NX) % NX * nz + (z + dz) % nz
    packed = jnp.zeros((n_row, LANES), jnp.int32)
    for i in range(CAP):
        hit = (to == dest) & (rank == i)
        which = jnp.sum(jnp.where(hit, lane, 0), axis=1, keepdims=True)
        tag = jnp.sum(jnp.where(hit, label, 0), axis=1, keepdims=True)
        packed = jnp.where(lane == i, which, jnp.where(lane == CAP + i, tag, packed))
    pack[...] = packed
    fetch = pltpu.make_async_copy(pack, pack_s, local_sem.at[0])
    fetch.start()

    def set_label(q, carry):
        lab_send[q] = pack[pl.ds(q, 1), :]
        return carry

    lax.fori_loop(0, n_row, set_label, 0)
    lab_recv[0] = lab_send[0]

    pl.semaphore_wait(barrier, n_row - 1 + 3)

    def label_copy(q):
        return pltpu.make_async_remote_copy(
            src_ref=lab_send.at[q], dst_ref=lab_recv.at[q], send_sem=lab_ss.at[q], recv_sem=lab_rs.at[q],
            device_id=(owner(q), split), device_id_type=MESH,
        )

    def tile_copy(q):
        return pltpu.make_async_remote_copy(
            src_ref=send.at[q], dst_ref=recv.at[q], send_sem=tile_ss.at[q], recv_sem=tile_rs.at[q],
            device_id=(owner(q), split), device_id_type=MESH,
        )

    def send_label(q, carry):
        label_copy(q).start()
        return carry

    lax.fori_loop(1, n_row, send_label, 0)
    fetch.wait()

    def send_tiles(q, carry):
        for i in range(CAP):
            send[q, pl.ds(i * ROWS, ROWS), :] = tiles_ref[pack_s[q, i]]
        tile_copy(q).start()
        return carry

    lax.fori_loop(1, n_row, send_tiles, 0)
    for i in range(CAP):
        recv[0, pl.ds(i * ROWS, ROWS), :] = tiles_ref[pack_s[0, i]]

    def wait_label(q, carry):
        label_copy(q).wait_recv()
        return carry

    lax.fori_loop(1, n_row, wait_label, 0)
    for q in range(n_row):
        pack[q:q + 1, :] = lab_recv[q]
    labels = pack[...]
    nothing = slots
    rows_of, cols_of, across = [], [], []
    for i in range(CAP):
        tag = jnp.sum(jnp.where(lane == CAP + i, labels, 0), axis=1, keepdims=True) - 1
        rows_of.append(tag >> 4)
        cols_of.append(tag & 15)
        across.append(jnp.sum(jnp.where(lane == q_sub, rows_of[i], 0), axis=0, keepdims=True))
    planned = jnp.zeros((n_row, LANES), jnp.int32)
    last = jnp.full((n_row, LANES), -1, jnp.int32)
    for i in range(CAP):
        best = jnp.full((n_row, LANES), -1, jnp.int32)
        for h in range(CAP):
            earlier = (lane <= q_sub) if h < i else (lane < q_sub)
            best = jnp.maximum(best, jnp.where(earlier & (rows_of[i] == across[h]), lane * CAP + h, -1))
        before = jnp.max(best, axis=1, keepdims=True)
        before = jnp.where(before < 0, nothing, before)
        planned = jnp.where(lane == i, before, jnp.where(lane == CAP + i, cols_of[i], planned))
        last = jnp.maximum(last, jnp.where(rows_of[i] == lane, q_sub * CAP + i, -1))
    last = jnp.max(last, axis=0, keepdims=True)
    plan[0:n_row, :] = planned
    plan[n_row:n_row + 8, :] = jnp.broadcast_to(jnp.where(last < 0, nothing, last), (8, LANES))
    fetch_plan = pltpu.make_async_copy(plan, plan_s, local_sem.at[1])
    fetch_plan.start()
    sums[nothing] = jnp.zeros((B, sums.shape[2]), jnp.float32)
    fetch_plan.wait()

    def work(q):
        products = []
        for i in range(CAP):
            block = recv[q, pl.ds(i * ROWS, ROWS), :]
            lhs = jnp.concatenate([block[:, :B], block[:, B:]], axis=0)
            products.append(jnp.dot(lhs, dens_ref[plan_s[q, CAP + i]], preferred_element_type=jnp.float32))
        for i in range(CAP):
            sums[q * CAP + i] = products[i] + sums[plan_s[q, i]]

    work(0)

    def turn(q, carry):
        tile_copy(q).wait_recv()
        work(q)
        return carry

    lax.fori_loop(1, n_row, turn, 0)

    def partial(ahead, c, b):
        g = (shift(y, ahead, ny) * 2 + c) * 2 + b
        return sums[plan_s[n_row, g]]

    def x_copy(ahead):
        return pltpu.make_async_remote_copy(
            src_ref=xsend.at[ahead], dst_ref=xrecv.at[ahead], send_sem=x_ss.at[ahead], recv_sem=x_rs.at[ahead],
            device_id=other, device_id_type=MESH,
        )

    order = [half]
    for t in range(1, half):
        order += [half - t, half + t]
    order += [0]
    for ahead in order:
        for b in range(2):
            xsend[ahead, b] = partial(ahead, 1 - core, b)
        x_copy(ahead).start()

    def u_copy(t, b):
        return pltpu.make_async_remote_copy(
            src_ref=usend.at[t, b], dst_ref=urecv.at[t, b], send_sem=u_ss.at[t, b], recv_sem=u_rs.at[t, b],
            device_id=above, device_id_type=MESH,
        )

    def d_copy(t, b):
        return pltpu.make_async_remote_copy(
            src_ref=dsend.at[t, b], dst_ref=drecv.at[t, b], send_sem=d_ss.at[t, b], recv_sem=d_rs.at[t, b],
            device_id=below, device_id_type=MESH,
        )

    def mine(ahead, b):
        return partial(ahead, core, b) + xrecv[ahead, b]

    sent = []
    x_copy(half).wait_recv()
    usend[0, 0] = mine(half, 0)
    u_copy(0, 0).start()
    dsend[0, 1] = mine(half, 1)
    d_copy(0, 1).start()
    sent += [u_copy(0, 0), d_copy(0, 1)]
    for t in range(1, half):
        x_copy(half - t).wait_recv()
        x_copy(half + t).wait_recv()
        for step in range(2):
            b = step
            term = mine(half - t, b)
            if t > 1 or b == 0:
                u_copy(t - 1, b).wait_recv()
                term = term + urecv[t - 1, b]
            usend[t, b] = term
            u_copy(t, b).start()
            b = 1 - step
            term = mine(half + t, b)
            if t > 1 or b == 1:
                d_copy(t - 1, b).wait_recv()
                term = term + drecv[t - 1, b]
            dsend[t, b] = term
            d_copy(t, b).start()
            sent += [u_copy(t, step), d_copy(t, b)]
    x_copy(0).wait_recv()
    to_row = lax.broadcasted_iota(jnp.int32, (B, B), 0)
    from_row = lax.broadcasted_iota(jnp.int32, (B, B), 1)
    swap = (from_row == to_row % 2 * ROWS + to_row // 2).astype(jnp.bfloat16)
    for b in range(2):
        total = mine(0, b)
        if half > 1 or b == 0:
            u_copy(half - 1, b).wait_recv()
            total = total + urecv[half - 1, b]
        if half > 1 or b == 1:
            d_copy(half - 1, b).wait_recv()
            total = total + drecv[half - 1, b]
        rounded = total.astype(jnp.bfloat16)
        out_ref[pl.ds(b * B, B), :] = jnp.dot(
            swap, rounded, preferred_element_type=jnp.float32
        ).astype(jnp.bfloat16)

    def finish(q, carry):
        label_copy(q).wait_send()
        tile_copy(q).wait_send()
        return carry

    lax.fori_loop(1, n_row, finish, 0)
    for ahead in order:
        x_copy(ahead).wait_send()
    for copy in sent:
        copy.wait_send()


def on_device(n_row, n_split, tiles, tile_dest, tile_row, tile_col, density):
    count, orbitals = tiles.shape[0], density.shape[1]
    ny = n_split // 2
    half = ny // 2
    label = 1 + tile_row * 16 + tile_col
    meta = jnp.stack([tile_dest[:, 0], label])
    meta = jnp.pad(meta, ((0, 0), (0, LANES - count)), constant_values=-1)
    blocks = tiles.reshape(count, ROWS, LANES)
    vmem = pl.BlockSpec(memory_space=pltpu.VMEM)
    f32, i32, bf16 = jnp.float32, jnp.int32, jnp.bfloat16
    dma = pltpu.SemaphoreType.DMA
    return pl.pallas_call(
        functools.partial(kernel, n_row, n_split),
        out_shape=jax.ShapeDtypeStruct((2 * B, orbitals), bf16),
        in_specs=[vmem] * 3,
        out_specs=vmem,
        scratch_shapes=[
            pltpu.VMEM((n_row, LANES), i32),
            pltpu.SMEM((n_row, LANES), i32),
            pltpu.VMEM((n_row, CAP * ROWS, LANES), bf16),
            pltpu.VMEM((n_row, CAP * ROWS, LANES), bf16),
            pltpu.VMEM((n_row, 1, LANES), i32),
            pltpu.VMEM((n_row, 1, LANES), i32),
            pltpu.VMEM((n_row + 8, LANES), i32),
            pltpu.SMEM((n_row + 8, LANES), i32),
            pltpu.VMEM((n_row * CAP + 1, B, orbitals), f32),
            pltpu.VMEM((ny, 2, B, orbitals), f32),
            pltpu.VMEM((ny, 2, B, orbitals), f32),
            pltpu.VMEM((half, 2, B, orbitals), f32),
            pltpu.VMEM((half, 2, B, orbitals), f32),
            pltpu.VMEM((half, 2, B, orbitals), f32),
            pltpu.VMEM((half, 2, B, orbitals), f32),
            dma((2,)), dma((n_row,)), dma((n_row,)), dma((n_row,)), dma((n_row,)),
            dma((ny,)), dma((ny,)), dma((half, 2)), dma((half, 2)), dma((half, 2)), dma((half, 2)),
        ],
        compiler_params=pltpu.CompilerParams(
            collective_id=0, has_side_effects=True, vmem_limit_bytes=40 * 2**20
        ),
        cost_estimate=pl.CostEstimate(
            flops=2 * n_row * CAP * B * B * orbitals, bytes_accessed=tiles.size * 2, transcendentals=0
        ),
    )(meta, blocks, density.reshape(-1, B, orbitals))


def solution(mesh):
    n_row, n_split = mesh.shape["row"], mesh.shape["split"]
    placed = (
        P(("row", "split"), None),
        P(("row", "split"), None),
        P(("row", "split")),
        P(("row", "split")),
        P("split", None),
    )
    return jax.shard_map(
        functools.partial(on_device, n_row, n_split),
        mesh=mesh, in_specs=placed, out_specs=P(("row", "split"), None), check_vma=False,
    )
```

time: 277 us -> 88.5 us (0.32)
  waiting for transfers between devices: 116 us -> 0 us
  Pallas kernels: 0 us -> 85 us
  other arithmetic: 59.6 us -> 0.01 us
  local copies, waits for them, and re-layouts: 44.6 us -> 3.31 us
  starting transfers between devices: 30.8 us -> 0 us
  between operations: 13.5 us -> 0.04 us
  matrix products: 10.9 us -> 0 us
    pallas_call x0 -> x1, Pallas kernels: none -> 85 us  [on_device(): pl.pallas_call(functools.partial(kernel, n_row, n_split), out_shape=jax.S...]
    reduce_scatter x1 -> x0, waiting for transfers between devices: 64.1 us -> none  [on_device(): lax.psum_scatter(partial_rows, 'split', scatter_dimension=0, tiled=True)]
    scatter-add x3 -> x0, other arithmetic: 54.6 us -> none  [add_group(): part.at[place.reshape(-1)].add(product.reshape(-1, orbitals), mode='drop')]
    all_to_all x2 -> x0, waiting for transfers between devices: 52.3 us -> none  [the longest x1 52.3 us: on_device(): lax.all_to_all(send_tiles, 'row', split_axis=0, concat_axis=0, tiled=True)]
    all_to_all x2 -> x0, starting transfers between devices: 30.8 us -> none  [the longest x1 18.8 us: on_device(): lax.all_to_all(send_labels, 'row', split_axis=0, concat_axis=0, tiled=True)]
    scatter x4 -> x0, local copies, waits for them, and re-layouts: 23.1 us -> none  [the longest x2 16.7 us: on_device(): jnp.zeros((owners, capacity, flat), jnp.bfloat16).at[target, slot]]
    dot_general x3 -> x0, matrix products: 10.9 us -> none  [add_group(): jnp.einsum('sab,sbo->sao', group_tiles, picked, preferred_element_type=jn...]
    gather x3 -> x0, local copies, waits for them, and re-layouts: 5.55 us -> none  [add_group(): picked = dens_blocks[jnp.clip(group_cols, 0, nublocks - 1)]]
  transfers between devices with their start and end apart: 3 -> 0, of which waited for: 2 -> 0; matrix products, arithmetic and copies ran while one was open for 6% -> 0% of each run, Pallas kernels for 0% -> 0%
where the time goes in v1:
time: 88.5 us; the launch traced here: 88.3 us
  Pallas kernels  85 us (96%)
  local copies, waits for them, and re-layouts  3.31 us (4%)
    pallas_call x1, Pallas kernels, on_device(): pl.pallas_call(functools.partial(kernel, n_row, n_split), out_shape=jax.S...  85 us
    unnamed x10, local copies, waits for them, and re-layouts  3.3 us

profile of v1, /device:TPU:1, one launch (start us, length us, event | category | flops | bytes accessed | tf_op | source)
XLA Modules:
  0.0 88.3 jit_solution(4215383597426134706)
XLA Ops:
  0.0 0.0 copy-start.2
  0.0 0.0 copy-start.3
  0.0 0.7 copy-done.2
  0.7 0.0 copy-done.3
  0.7 0.0 copy-start.1
  0.7 0.6 copy-done.1
  1.3 0.0 copy-start
  1.4 1.3 %copy.6 = bf16[12,8,32,128]{3,2,1,0:T(8,128)(2,1)S(1)} copy(bf16[12,8,32,128]{3,1,2,0:T(8,128)(2,1)} %bitcast.8) | data formatting | bytes 1572864
  2.7 0.0 copy-done
  2.7 85.0 %shard_map.55 = bf16[128,256]{1,0:T(8,128)(2,1)S(1)} custom-call(s32[2,128]{1,0:T(2,128)S(1)} %pad.4.meta_ref, bf16[96,32,128]{2,1,0:T(8,128)(2,1)S(1)} %bitcast.6, bf16[16,64,256]{2,1,0:T(8,128)(2,1)S(1)} %bitcast.7), custom_call_target="tpu_custom_call" | custom-call | flops 301989888 | bytes 786432 | tf_op jit(solution)/shard_map/pallas_call | solution.py:272
  87.7 0.6 copy.8
  (3 shorter events, 0.0 us)
Async XLA Ops:
  0.0 0.7 copy-start.2
  0.0 0.7 copy-start.3
  0.7 0.7 copy-start.1
  1.3 1.4 %copy-start = (bf16[1024,256]{1,0:T(8,128)(2,1)S(1)}, bf16[1024,256]{1,0:T(8,128)(2,1)}, u32[]{:S(2)}) copy-start(bf16[1024,256]{1,0:T(8,128)(2,1)} %param.9) | copy-start | bytes 1572868

commit v2 on v1

v2 whole, which is shorter than its diff:
```python
import functools

import jax
import jax.numpy as jnp
from jax import lax
from jax.experimental import pallas as pl
from jax.experimental.pallas import tpu as pltpu
from jax.sharding import PartitionSpec as P

MESH = pl.DeviceIdType.MESH
B = 64
LANES = 128
ROWS = B * B // LANES
CAP = 3
NX = 4


def shift(at, by, size):
    return lax.rem(at + by, size)


def kernel(
    n_row, n_split, dest_hbm, row_hbm, col_hbm, tiles_hbm, dens_hbm, out_ref,
    dest_v, row_v, col_v, tiles_v, dens_ref, tall,
    pack, pack_s, send, recv, lab_send, lab_recv, plan, plan_s, sums,
    xsend, xrecv, usend0, urecv0, dsend0, drecv0, usend, urecv, dsend, drecv,
    local_sem, lab_ss, lab_rs, tile_ss, tile_rs, x_ss, x_rs,
    u0_ss, u0_rs, d0_ss, d0_rs, u_ss, u_rs, d_ss, d_rs,
):
    nz, ny = n_row // NX, n_split // 2
    half = ny // 2
    slots = n_row * CAP
    row, split = lax.axis_index("row"), lax.axis_index("split")
    x, z = row // nz, lax.rem(row, nz)
    y, core = split // 2, lax.rem(split, 2)
    up_y, down_y = shift(y, 1, ny) * 2, shift(y, ny - 1, ny) * 2
    other = (row, y * 2 + 1 - core)
    above, above_other = (row, up_y + core), (row, up_y + 1 - core)
    below, below_other = (row, down_y + core), (row, down_y + 1 - core)

    def offset(q):
        u = (n_row - q) % n_row
        k = u // NX
        odd = k % 2
        return u % NX, odd * ((k + 1) // 2) + (1 - odd) * ((nz - k // 2) % nz)

    def owner(q):
        dx, dz = offset(q)
        return (x + dx) % NX * nz + (z + dz) % nz

    fetches = []
    for i, (src, dst) in enumerate(
        [(dest_hbm, dest_v), (row_hbm, row_v), (col_hbm, col_v), (tiles_hbm, tiles_v), (dens_hbm, dens_ref)]
    ):
        fetches.append(pltpu.make_async_copy(src, dst, local_sem.at[2 + i]))
        fetches[i].start()

    barrier = pltpu.get_barrier_semaphore()

    def greet(q, carry):
        pl.semaphore_signal(barrier, inc=1, device_id=(owner(q), split), device_id_type=MESH)
        return carry

    lax.fori_loop(1, n_row, greet, 0)
    for peer in (other, above, above_other, below, below_other):
        pl.semaphore_signal(barrier, inc=1, device_id=peer, device_id_type=MESH)

    for i in range(3):
        fetches[i].wait()
    dest = dest_v[...]
    label = 1 + row_v[...] * 16 + col_v[...]
    width = dest.shape[1]
    t_sub = lax.broadcasted_iota(jnp.int32, (width, width), 0)
    t_lane = lax.broadcasted_iota(jnp.int32, (width, width), 1)
    dest_col = jnp.sum(jnp.where(t_sub == t_lane, dest, 0), axis=1, keepdims=True)
    rank = jnp.sum(jnp.where((dest_col == dest) & (t_sub < t_lane), 1, 0), axis=0, keepdims=True)
    q_sub = lax.broadcasted_iota(jnp.int32, (n_row, LANES), 0)
    lane = lax.broadcasted_iota(jnp.int32, (n_row, LANES), 1)
    t_of = lax.broadcasted_iota(jnp.int32, (n_row, width), 1)
    q_of = lax.broadcasted_iota(jnp.int32, (n_row, 1), 0)
    u = jnp.where(q_of == 0, 0, n_row - q_of)
    k = u // NX
    dz = jnp.where(k % 2 == 1, (k + 1) // 2, (nz - k // 2) % nz)
    to = (x + u % NX) % NX * nz + (z + dz) % nz
    packed = jnp.zeros((n_row, LANES), jnp.int32)
    for i in range(CAP):
        hit = (to == dest) & (rank == i)
        which = jnp.sum(jnp.where(hit, t_of, 0), axis=1, keepdims=True)
        tag = jnp.sum(jnp.where(hit, label, 0), axis=1, keepdims=True)
        packed = jnp.where(lane == i, which, jnp.where(lane == CAP + i, tag, packed))
    pack[...] = packed
    fetch = pltpu.make_async_copy(pack, pack_s, local_sem.at[0])
    fetch.start()

    fetches[3].wait()
    def lay(g, carry):
        group = tiles_v[g].astype(jnp.float32)
        for p in range(ROWS):
            tall[pl.ds(g * 8, 8), p, :] = group[p]
        return carry

    lax.fori_loop(0, tiles_v.shape[0], lay, 0)

    def set_label(q, carry):
        lab_send[q] = pack[pl.ds(q, 1), :]
        return carry

    lax.fori_loop(0, n_row, set_label, 0)
    lab_recv[0] = lab_send[0]
    fetch.wait()

    pl.semaphore_wait(barrier, n_row - 1 + 5)

    def label_copy(q):
        return pltpu.make_async_remote_copy(
            src_ref=lab_send.at[q], dst_ref=lab_recv.at[q], send_sem=lab_ss.at[q], recv_sem=lab_rs.at[q],
            device_id=(owner(q), split), device_id_type=MESH,
        )

    def tile_copy(q):
        return pltpu.make_async_remote_copy(
            src_ref=send.at[q], dst_ref=recv.at[q], send_sem=tile_ss.at[q], recv_sem=tile_rs.at[q],
            device_id=(owner(q), split), device_id_type=MESH,
        )

    def send_label(q, carry):
        label_copy(q).start()
        return carry

    def send_tiles(q, carry):
        for i in range(CAP):
            send[q, pl.ds(i * ROWS, ROWS), :] = tall[pack_s[q, i]].astype(jnp.bfloat16)
        tile_copy(q).start()
        return carry

    ahead_of_labels = min(9, n_row)
    lax.fori_loop(1, ahead_of_labels, send_tiles, 0)
    lax.fori_loop(1, n_row, send_label, 0)
    lax.fori_loop(ahead_of_labels, n_row, send_tiles, 0)
    for i in range(CAP):
        recv[0, pl.ds(i * ROWS, ROWS), :] = tall[pack_s[0, i]].astype(jnp.bfloat16)

    def wait_label(q, carry):
        label_copy(q).wait_recv()
        return carry

    lax.fori_loop(1, n_row, wait_label, 0)
    for q in range(n_row):
        pack[q:q + 1, :] = lab_recv[q]
    labels = pack[...]
    nothing = slots
    rows_of, cols_of, across = [], [], []
    for i in range(CAP):
        tag = jnp.sum(jnp.where(lane == CAP + i, labels, 0), axis=1, keepdims=True) - 1
        rows_of.append(tag >> 4)
        cols_of.append(tag & 15)
        across.append(jnp.sum(jnp.where(lane == q_sub, rows_of[i], 0), axis=0, keepdims=True))
    planned = jnp.zeros((n_row, LANES), jnp.int32)
    last = jnp.full((n_row, LANES), -1, jnp.int32)
    for i in range(CAP):
        best = jnp.full((n_row, LANES), -1, jnp.int32)
        for h in range(CAP):
            earlier = (lane <= q_sub) if h < i else (lane < q_sub)
            best = jnp.maximum(best, jnp.where(earlier & (rows_of[i] == across[h]), lane * CAP + h, -1))
        before = jnp.max(best, axis=1, keepdims=True)
        before = jnp.where(before < 0, nothing, before)
        planned = jnp.where(lane == i, before, jnp.where(lane == CAP + i, cols_of[i], planned))
        last = jnp.maximum(last, jnp.where(rows_of[i] == lane, q_sub * CAP + i, -1))
    last = jnp.max(last, axis=0, keepdims=True)
    plan[0:n_row, :] = planned
    plan[n_row:n_row + 8, :] = jnp.broadcast_to(jnp.where(last < 0, nothing, last), (8, LANES))
    fetch_plan = pltpu.make_async_copy(plan, plan_s, local_sem.at[1])
    fetch_plan.start()
    sums[nothing] = jnp.zeros((B, sums.shape[2]), jnp.float32)
    fetch_plan.wait()
    fetches[4].wait()

    def work(q):
        products = []
        for i in range(CAP):
            block = recv[q, pl.ds(i * ROWS, ROWS), :]
            lhs = jnp.concatenate([block[:, :B], block[:, B:]], axis=0)
            products.append(jnp.dot(lhs, dens_ref[plan_s[q, CAP + i]], preferred_element_type=jnp.float32))
        for i in range(CAP):
            sums[q * CAP + i] = products[i] + sums[plan_s[q, i]]

    work(0)

    def turn(q, carry):
        tile_copy(q).wait_recv()
        work(q)
        return carry

    lax.fori_loop(1, n_row, turn, 0)

    def partial(ahead, c, b):
        g = (shift(y, ahead, ny) * 2 + c) * 2 + b
        return sums[plan_s[n_row, g]]

    def remote(src, dst, ss, rs, to):
        return pltpu.make_async_remote_copy(
            src_ref=src, dst_ref=dst, send_sem=ss, recv_sem=rs, device_id=to, device_id_type=MESH
        )

    def first(way, c, h):
        if way == 0:
            return remote(usend0.at[c, h], urecv0.at[c, h], u0_ss.at[c, h], u0_rs.at[c, h], (above, above_other)[c])
        return remote(dsend0.at[c, h], drecv0.at[c, h], d0_ss.at[c, h], d0_rs.at[c, h], (below, below_other)[c])

    def later(way, t, b, h):
        if way == 0:
            return remote(usend.at[t, b, h], urecv.at[t, b, h], u_ss.at[t, b, h], u_rs.at[t, b, h], above)
        return remote(dsend.at[t, b, h], drecv.at[t, b, h], d_ss.at[t, b, h], d_rs.at[t, b, h], below)

    def x_copy(ahead):
        return remote(xsend.at[ahead], xrecv.at[ahead], x_ss.at[ahead], x_rs.at[ahead], other)

    sent = []

    def go(copy):
        copy.start()
        sent.append(copy)

    for c in range(2):
        shares = [partial(half, (core, 1 - core)[c], way) for way in range(2)]
        for h in range(2):
            for way in range(2):
                (usend0, dsend0)[way][c, h] = shares[way][h * ROWS:(h + 1) * ROWS]
                go(first(way, c, h))
    order = []
    for t in range(1, half):
        order += [half - t, half + t]
    order += [0]
    for ahead in order:
        for b in range(2):
            xsend[ahead, b] = partial(ahead, 1 - core, b)
        go(x_copy(ahead))

    def finish(q, carry):
        label_copy(q).wait_send()
        tile_copy(q).wait_send()
        return carry

    lax.fori_loop(1, n_row, finish, 0)

    def came(way, t, b, h):
        if t == 0:
            if way != b:
                return 0.0
            got = 0.0
            for c in range(2):
                first(way, c, h).wait_recv()
                got = got + (urecv0, drecv0)[way][c, h]
            return got
        later(way, t, b, h).wait_recv()
        return (urecv, drecv)[way][t, b, h]

    for t in range(1, half):
        x_copy(half - t).wait_recv()
        x_copy(half + t).wait_recv()
        for step in range(2):
            for way, b in ((0, 1 - step), (1, step)):
                ahead = half - t if way == 0 else half + t
                term = partial(ahead, core, b) + xrecv[ahead, b]
                for h in range(2):
                    (usend, dsend)[way][t, b, h] = term[h * ROWS:(h + 1) * ROWS] + came(way, t - 1, b, h)
                    go(later(way, t, b, h))
    x_copy(0).wait_recv()
    to_row = lax.broadcasted_iota(jnp.int32, (B, B), 0)
    from_row = lax.broadcasted_iota(jnp.int32, (B, B), 1)
    swap = (from_row == to_row % 2 * ROWS + to_row // 2).astype(jnp.bfloat16)
    for b in range(2):
        term = partial(0, core, b) + xrecv[0, b]
        halves = []
        for h in range(2):
            total = term[h * ROWS:(h + 1) * ROWS] + came(0, half - 1, b, h) + came(1, half - 1, b, h)
            halves.append(total.astype(jnp.bfloat16))
        out_ref[pl.ds(b * B, B), :] = jnp.dot(
            swap, jnp.concatenate(halves, axis=0), preferred_element_type=jnp.float32
        ).astype(jnp.bfloat16)
    for copy in sent:
        copy.wait_send()


def on_device(n_row, n_split, tiles, tile_dest, tile_row, tile_col, density):
    count, orbitals = tiles.shape[0], density.shape[1]
    ny = n_split // 2
    half = ny // 2
    groups = tiles.reshape(count // 8, 8, ROWS, LANES).transpose(0, 2, 1, 3)
    vmem = pl.BlockSpec(memory_space=pltpu.VMEM)
    hbm = pl.BlockSpec(memory_space=pltpu.HBM)
    f32, i32, bf16 = jnp.float32, jnp.int32, jnp.bfloat16
    dma = pltpu.SemaphoreType.DMA
    return pl.pallas_call(
        functools.partial(kernel, n_row, n_split),
        out_shape=jax.ShapeDtypeStruct((2 * B, orbitals), bf16),
        in_specs=[hbm] * 5,
        out_specs=vmem,
        scratch_shapes=[
            pltpu.VMEM((1, count), i32),
            pltpu.VMEM((1, count), i32),
            pltpu.VMEM((1, count), i32),
            pltpu.VMEM(groups.shape, bf16),
            pltpu.VMEM((density.shape[0] // B, B, orbitals), bf16),
            pltpu.VMEM((count, ROWS, LANES), f32),
            pltpu.VMEM((n_row, LANES), i32),
            pltpu.SMEM((n_row, LANES), i32),
            pltpu.VMEM((n_row, CAP * ROWS, LANES), bf16),
            pltpu.VMEM((n_row, CAP * ROWS, LANES), bf16),
            pltpu.VMEM((n_row, 1, LANES), i32),
            pltpu.VMEM((n_row, 1, LANES), i32),
            pltpu.VMEM((n_row + 8, LANES), i32),
            pltpu.SMEM((n_row + 8, LANES), i32),
            pltpu.VMEM((n_row * CAP + 1, B, orbitals), f32),
            pltpu.VMEM((ny, 2, B, orbitals), f32),
            pltpu.VMEM((ny, 2, B, orbitals), f32),
            *[pltpu.VMEM((2, 2, ROWS, orbitals), f32)] * 4,
            *[pltpu.VMEM((half, 2, 2, ROWS, orbitals), f32)] * 4,
            dma((7,)), *[dma((n_row,))] * 4, *[dma((ny,))] * 2, *[dma((2, 2))] * 4, *[dma((half, 2, 2))] * 4,
        ],
        compiler_params=pltpu.CompilerParams(
            collective_id=0, has_side_effects=True, vmem_limit_bytes=63 * 2**20
        ),
        cost_estimate=pl.CostEstimate(
            flops=2 * n_row * CAP * B * B * orbitals, bytes_accessed=tiles.size * 2, transcendentals=0
        ),
    )(
        tile_dest.reshape(1, count), tile_row.reshape(1, count), tile_col.reshape(1, count), groups,
        density.reshape(-1, B, orbitals),
    )


def solution(mesh):
    n_row, n_split = mesh.shape["row"], mesh.shape["split"]
    placed = (
        P(("row", "split"), None),
        P(("row", "split"), None),
        P(("row", "split")),
        P(("row", "split")),
        P("split", None),
    )
    return jax.shard_map(
        functools.partial(on_device, n_row, n_split),
        mesh=mesh, in_specs=placed, out_specs=P(("row", "split"), None), check_vma=False,
    )
```

time: 88.5 us -> 83 us (0.938)
  Pallas kernels: 85 us -> 81.2 us
  local copies, waits for them, and re-layouts: 3.31 us -> 1.47 us
    pallas_call x1, Pallas kernels: 85 us -> 81.2 us  [on_device(): pl.pallas_call(functools.partial(kernel, n_row, n_split), out_shape=jax.S...]
    unnamed x10 -> x1, local copies, waits for them, and re-layouts: 3.3 us -> 1.47 us
where the time goes in v2:
time: 83 us; the launch traced here: 82.7 us
  Pallas kernels  81.2 us (98%)
  local copies, waits for them, and re-layouts  1.47 us (2%)
    pallas_call x1, Pallas kernels, on_device(): pl.pallas_call(functools.partial(kernel, n_row, n_split), out_shape=jax.S...  81.2 us

profile of v2, /device:TPU:1, one launch (start us, length us, event | category | flops | bytes accessed | tf_op | source)
XLA Modules:
  0.0 82.7 jit_solution(12922076846043648882)
XLA Ops:
  0.0 81.2 %shard_map.55 = bf16[128,256]{1,0:T(8,128)(2,1)} custom-call(s32[1,96]{1,0:T(1,128)} %bitcast.9, s32[1,96]{1,0:T(1,128)} %bitcast.10, s32[1,96]{1,0:T(1,128)} %bitcast.11, bf16[12,32,8,128]{3,2,1,0:T(8,128)(2,1)} %bitcast.7, bf16[16,64,256]{2,1,0:T(8,128)(2,1)} %bitcast.8), custom_call_target="tpu_custom_call" | custom-call | flops 301989888 | bytes 786432 | tf_op jit(solution)/shard_map/pallas_call | solution.py:294
  81.3 1.5 %copy.7 = bf16[128,256]{1,0:T(8,128)(2,1)} copy(bf16[128,256]{1,0:T(8,128)(2,1)} %shard_map.55) | data formatting | bytes 131072

commit v3 on v2

v3 whole, which is shorter than its diff:
```python
import functools

import jax
import jax.numpy as jnp
from jax import lax
from jax.experimental import pallas as pl
from jax.experimental.pallas import tpu as pltpu
from jax.sharding import PartitionSpec as P

MESH = pl.DeviceIdType.MESH
B = 64
LANES = 128
ROWS = B * B // LANES
CAP = 3
NX = 4


def shift(at, by, size):
    return lax.rem(at + by, size)


def kernel(
    n_row, n_split, dest_hbm, row_hbm, col_hbm, tiles_hbm, dens_hbm, out_ref,
    dest_v, row_v, col_v, tiles_v, dens_ref, tall,
    pack, pack_s, send, recv, lab_send, lab_recv, plan, plan_s, sums,
    xsend, xrecv, first_send, first_recv, later_send, later_recv, back_send, back_recv,
    local_sem, lab_ss, lab_rs, tile_ss, tile_rs, x_ss, x_rs,
    first_ss, first_rs, later_ss, later_rs, back_ss, back_rs,
):
    nz, ny = n_row // NX, n_split // 2
    half, opposite = ny // 2, nz // 2
    places = n_row // 2
    row, split = lax.axis_index("row"), lax.axis_index("split")
    x, z = row // nz, lax.rem(row, nz)
    y, core = split // 2, lax.rem(split, 2)
    up_y, down_y = shift(y, 1, ny) * 2, shift(y, ny - 1, ny) * 2
    other = (row, y * 2 + 1 - core)
    above, above_other = (row, up_y + core), (row, up_y + 1 - core)
    below, below_other = (row, down_y + core), (row, down_y + 1 - core)

    def at_row(dx, dz):
        return shift(x, dx, NX) * nz + shift(z, dz, nz)

    def place(q, x_of, z_of):
        u = (places - q) % places
        k = u // NX
        odd = k % 2
        px = (x_of + u % NX) % NX
        dz = odd * ((k + 1) // 2) + (1 - odd) * (nz - k // 2)
        flip = (k // (opposite - 1)) * (px % 2) if opposite > 1 else 0
        dz = dz + flip * (nz - 2 * dz)
        return px, (z_of + dz) % nz

    def device(q):
        px, pz = place(q, x, z)
        return px * nz + pz, split

    fetches = []
    for i, (src, dst) in enumerate(
        [(dest_hbm, dest_v), (row_hbm, row_v), (col_hbm, col_v), (tiles_hbm, tiles_v), (dens_hbm, dens_ref)]
    ):
        fetches.append(pltpu.make_async_copy(src, dst, local_sem.at[2 + i]))
        fetches[i].start()

    barrier = pltpu.get_barrier_semaphore()
    reach = opposite // 2
    near = {(dx, dz % nz) for dx in range(NX) for dz in range(-reach, reach + 1)} | {(0, opposite)}
    near = sorted(near - {(0, 0)})
    for dx, dz in near:
        pl.semaphore_signal(barrier, inc=1, device_id=(at_row(dx, dz), split), device_id_type=MESH)
    for peer in (other, above, above_other, below, below_other):
        pl.semaphore_signal(barrier, inc=1, device_id=peer, device_id_type=MESH)

    for i in range(3):
        fetches[i].wait()
    dest = dest_v[...]
    label = 1 + row_v[...] * 16 + col_v[...]
    width = dest.shape[1]
    t_sub = lax.broadcasted_iota(jnp.int32, (width, width), 0)
    t_lane = lax.broadcasted_iota(jnp.int32, (width, width), 1)
    dest_col = jnp.sum(jnp.where(t_sub == t_lane, dest, 0), axis=1, keepdims=True)
    rank = jnp.sum(jnp.where((dest_col == dest) & (t_sub < t_lane), 1, 0), axis=0, keepdims=True)
    q_sub = lax.broadcasted_iota(jnp.int32, (places, LANES), 0)
    lane = lax.broadcasted_iota(jnp.int32, (places, LANES), 1)
    t_of = lax.broadcasted_iota(jnp.int32, (places, width), 1)
    q_of = lax.broadcasted_iota(jnp.int32, (places, 1), 0)
    px, pz = place(q_of, x, z)
    packed = jnp.zeros((places, LANES), jnp.int32)
    for i in range(2 * CAP):
        to = px * nz + ((pz + opposite) % nz if i < CAP else pz)
        hit = (to == dest) & (rank == i % CAP)
        which = jnp.sum(jnp.where(hit, t_of, 0), axis=1, keepdims=True)
        tag = jnp.sum(jnp.where(hit, label, 0), axis=1, keepdims=True)
        packed = jnp.where(lane == i, which, jnp.where(lane == 2 * CAP + i, tag, packed))
    pack[...] = packed
    fetch = pltpu.make_async_copy(pack, pack_s, local_sem.at[0])
    fetch.start()

    fetches[3].wait()

    def lay(g, carry):
        group = tiles_v[g].astype(jnp.float32)
        for p in range(ROWS):
            tall[pl.ds(g * 8, 8), p, :] = group[p]
        return carry

    lax.fori_loop(0, tiles_v.shape[0], lay, 0)

    def set_label(q, carry):
        lab_send[q] = pack[pl.ds(q, 1), :]
        return carry

    lax.fori_loop(0, places, set_label, 0)
    lab_recv[0] = lab_send[0]
    fetch.wait()

    pl.semaphore_wait(barrier, len(near) + 5)

    def remote(src, dst, ss, rs, to):
        return pltpu.make_async_remote_copy(
            src_ref=src, dst_ref=dst, send_sem=ss, recv_sem=rs, device_id=to, device_id_type=MESH
        )

    def label_copy(q):
        return remote(lab_send.at[q], lab_recv.at[q], lab_ss.at[q], lab_rs.at[q], device(q))

    def tile_copy(part, q):
        return remote(send.at[part, q], recv.at[part, q], tile_ss.at[part, q], tile_rs.at[part, q], device(q))

    def send_label(q, carry):
        label_copy(q).start()
        return carry

    def blocks_to(ref, part, q):
        for i in range(CAP):
            ref[part, q, pl.ds(i * ROWS, ROWS), :] = tall[pack_s[q, part * CAP + i]].astype(jnp.bfloat16)

    def send_tiles(part):
        def step(q, carry):
            blocks_to(send, part, q)
            tile_copy(part, q).start()
            return carry
        return step

    ahead_of_labels = min(9, places)
    lax.fori_loop(1, ahead_of_labels, send_tiles(0), 0)
    lax.fori_loop(1, places, send_label, 0)
    lax.fori_loop(ahead_of_labels, places, send_tiles(0), 0)
    for part in range(2):
        blocks_to(recv, part, 0)

    def wait_label(q, carry):
        label_copy(q).wait_recv()
        return carry

    lax.fori_loop(1, places, wait_label, 0)
    for q in range(places):
        pack[q:q + 1, :] = lab_recv[q]
    labels = pack[...]
    nothing = 2 * places * CAP
    planned = jnp.zeros((places, LANES), jnp.int32)
    last = jnp.full((places, LANES), -1, jnp.int32)
    for part in range(2):
        rows_of, cols_of, across = [], [], []
        for i in range(CAP):
            tag = jnp.sum(jnp.where(lane == (2 + part) * CAP + i, labels, 0), axis=1, keepdims=True) - 1
            rows_of.append(tag >> 4)
            cols_of.append(tag & 15)
            across.append(jnp.sum(jnp.where(lane == q_sub, rows_of[i], 0), axis=0, keepdims=True))
        base = part * places * CAP
        for i in range(CAP):
            best = jnp.full((places, LANES), -1, jnp.int32)
            for h in range(CAP):
                earlier = (lane <= q_sub) if h < i else (lane < q_sub)
                best = jnp.maximum(best, jnp.where(earlier & (rows_of[i] == across[h]), base + lane * CAP + h, -1))
            before = jnp.max(best, axis=1, keepdims=True)
            before = jnp.where(before < 0, nothing, before)
            at = part * CAP + i
            planned = jnp.where(lane == at, before, jnp.where(lane == 2 * CAP + at, cols_of[i], planned))
            here = (rows_of[i] >= 0) & (rows_of[i] + part * 2 * n_split == lane)
            last = jnp.maximum(last, jnp.where(here, base + q_sub * CAP + i, -1))
    last = jnp.max(last, axis=0, keepdims=True)
    plan[0:places, :] = planned
    plan[places:places + 8, :] = jnp.broadcast_to(jnp.where(last < 0, nothing, last), (8, LANES))
    fetch_plan = pltpu.make_async_copy(plan, plan_s, local_sem.at[1])
    fetch_plan.start()
    sums[nothing] = jnp.zeros((B, sums.shape[2]), jnp.float32)
    fetch_plan.wait()
    fetches[4].wait()

    def work(part, q):
        products = []
        for i in range(CAP):
            block = recv[part, q, pl.ds(i * ROWS, ROWS), :]
            lhs = jnp.concatenate([block[:, :B], block[:, B:]], axis=0)
            col = plan_s[q, (2 + part) * CAP + i]
            products.append(jnp.dot(lhs, dens_ref[col], preferred_element_type=jnp.float32))
        for i in range(CAP):
            sums[(part * places + q) * CAP + i] = products[i] + sums[plan_s[q, part * CAP + i]]

    def turns(part, start, stop):
        def turn(q, carry):
            tile_copy(part, q).wait_recv()
            work(part, q)
            if part == 0:
                send_tiles(1)(q, 0)
            return carry

        if start == 0:
            work(part, 0)
        lax.fori_loop(max(start, 1), stop, turn, 0)

    sent = []

    def go(copy):
        copy.start()
        sent.append(copy)

    order = []
    for t in range(1, half):
        order += [half - t, half + t]
    order += [0]

    def partial(part, ahead, c, b):
        g = (shift(y, ahead, ny) * 2 + c) * 2 + b
        return sums[plan_s[places, part * 2 * n_split + g]]

    def first(part, way, c, h):
        at = (part, way, c, h)
        to = ((above, above_other), (below, below_other))[way][c]
        return remote(first_send.at[at], first_recv.at[at], first_ss.at[at], first_rs.at[at], to)

    def later(part, way, t, b, h):
        at = (part, way, t, b, h)
        return remote(later_send.at[at], later_recv.at[at], later_ss.at[at], later_rs.at[at], (above, below)[way])

    def x_copy(part, ahead):
        at = (part, ahead)
        return remote(xsend.at[at], xrecv.at[at], x_ss.at[at], x_rs.at[at], other)

    def begin(part):
        for c in range(2):
            shares = [partial(part, half, (core, 1 - core)[c], way) for way in range(2)]
            for h in range(2):
                for way in range(2):
                    first_send[part, way, c, h] = shares[way][h * ROWS:(h + 1) * ROWS]
                    go(first(part, way, c, h))
        for ahead in order:
            for b in range(2):
                xsend[part, ahead, b] = partial(part, ahead, 1 - core, b)
            go(x_copy(part, ahead))

    def came(part, way, t, b, h):
        if t == 0:
            if way != b:
                return 0.0
            got = 0.0
            for c in range(2):
                first(part, way, c, h).wait_recv()
                got = got + first_recv[part, way, c, h]
            return got
        later(part, way, t, b, h).wait_recv()
        return later_recv[part, way, t, b, h]

    def forward(part, t):
        x_copy(part, half - t).wait_recv()
        x_copy(part, half + t).wait_recv()
        for step in range(2):
            for way, b in ((0, 1 - step), (1, step)):
                ahead = half - t if way == 0 else half + t
                term = partial(part, ahead, core, b) + xrecv[part, ahead, b]
                for h in range(2):
                    later_send[part, way, t, b, h] = term[h * ROWS:(h + 1) * ROWS] + came(part, way, t - 1, b, h)
                    go(later(part, way, t, b, h))

    def total(part, b, h):
        if b == 0 and h == 0:
            x_copy(part, 0).wait_recv()
        term = partial(part, 0, core, b) + xrecv[part, 0, b]
        return term[h * ROWS:(h + 1) * ROWS] + came(part, 0, half - 1, b, h) + came(part, 1, half - 1, b, h)

    def back(b, h):
        at = (b, h)
        return remote(back_send.at[at], back_recv.at[at], back_ss.at[at], back_rs.at[at], (at_row(0, opposite), split))

    turns(0, 0, places)
    begin(0)
    cuts = [places * i // half for i in range(half + 1)]
    for t in range(half):
        if t > 0:
            forward(0, t)
        turns(1, cuts[t], cuts[t + 1])
    begin(1)
    for b in range(2):
        for h in range(2):
            back_send[b, h] = total(0, b, h)
            go(back(b, h))
    for t in range(1, half):
        forward(1, t)

    def finish(q, carry):
        label_copy(q).wait_send()
        for part in range(2):
            tile_copy(part, q).wait_send()
        return carry

    lax.fori_loop(1, places, finish, 0)
    to_row = lax.broadcasted_iota(jnp.int32, (B, B), 0)
    from_row = lax.broadcasted_iota(jnp.int32, (B, B), 1)
    swap = (from_row == to_row % 2 * ROWS + to_row // 2).astype(jnp.bfloat16)
    for b in range(2):
        halves = []
        for h in range(2):
            whole = total(1, b, h)
            back(b, h).wait_recv()
            halves.append((whole + back_recv[b, h]).astype(jnp.bfloat16))
        out_ref[pl.ds(b * B, B), :] = jnp.dot(
            swap, jnp.concatenate(halves, axis=0), preferred_element_type=jnp.float32
        ).astype(jnp.bfloat16)
    for copy in sent:
        copy.wait_send()


def on_device(n_row, n_split, tiles, tile_dest, tile_row, tile_col, density):
    count, orbitals = tiles.shape[0], density.shape[1]
    places, ny = n_row // 2, n_split // 2
    half = ny // 2
    groups = tiles.reshape(count // 8, 8, ROWS, LANES).transpose(0, 2, 1, 3)
    hbm = pl.BlockSpec(memory_space=pltpu.HBM)
    f32, i32, bf16 = jnp.float32, jnp.int32, jnp.bfloat16
    vmem, smem, dma = pltpu.VMEM, pltpu.SMEM, pltpu.SemaphoreType.DMA
    return pl.pallas_call(
        functools.partial(kernel, n_row, n_split),
        out_shape=jax.ShapeDtypeStruct((2 * B, orbitals), bf16),
        in_specs=[hbm] * 5,
        out_specs=pl.BlockSpec(memory_space=vmem),
        scratch_shapes=[
            *[vmem((1, count), i32)] * 3,
            vmem(groups.shape, bf16),
            vmem((density.shape[0] // B, B, orbitals), bf16),
            vmem((count, ROWS, LANES), f32),
            vmem((places, LANES), i32),
            smem((places, LANES), i32),
            *[vmem((2, places, CAP * ROWS, LANES), bf16)] * 2,
            *[vmem((places, 1, LANES), i32)] * 2,
            vmem((places + 8, LANES), i32),
            smem((places + 8, LANES), i32),
            vmem((2 * places * CAP + 1, B, orbitals), f32),
            *[vmem((2, ny, 2, B, orbitals), f32)] * 2,
            *[vmem((2, 2, 2, 2, ROWS, orbitals), f32)] * 2,
            *[vmem((2, 2, half, 2, 2, ROWS, orbitals), f32)] * 2,
            *[vmem((2, 2, ROWS, orbitals), f32)] * 2,
            dma((7,)), *[dma((places,))] * 2, *[dma((2, places))] * 2, *[dma((2, ny))] * 2,
            *[dma((2, 2, 2, 2))] * 2, *[dma((2, 2, half, 2, 2))] * 2, *[dma((2, 2))] * 2,
        ],
        compiler_params=pltpu.CompilerParams(
            collective_id=0, has_side_effects=True, vmem_limit_bytes=63 * 2**20
        ),
        cost_estimate=pl.CostEstimate(
            flops=2 * n_row * CAP * B * B * orbitals, bytes_accessed=tiles.size * 2, transcendentals=0
        ),
    )(
        tile_dest.reshape(1, count), tile_row.reshape(1, count), tile_col.reshape(1, count), groups,
        density.reshape(-1, B, orbitals),
    )


def solution(mesh):
    n_row, n_split = mesh.shape["row"], mesh.shape["split"]
    placed = (
        P(("row", "split"), None),
        P(("row", "split"), None),
        P(("row", "split")),
        P(("row", "split")),
        P("split", None),
    )
    return jax.shard_map(
        functools.partial(on_device, n_row, n_split),
        mesh=mesh, in_specs=placed, out_specs=P(("row", "split"), None), check_vma=False,
    )
```

time: 83 us -> 72.1 us (0.87)
  Pallas kernels: 81.2 us -> 70.2 us
    pallas_call x1, Pallas kernels: 81.2 us -> 70.2 us  [on_device(): pl.pallas_call(functools.partial(kernel, n_row, n_split), out_shape=jax.S...]
where the time goes in v3:
time: 72.1 us; the launch traced here: 71.7 us
  Pallas kernels  70.2 us (97%)
  local copies, waits for them, and re-layouts  1.47 us (2%)
    pallas_call x1, Pallas kernels, on_device(): pl.pallas_call(functools.partial(kernel, n_row, n_split), out_shape=jax.S...  70.2 us
    unnamed x1, local copies, waits for them, and re-layouts  1.47 us

profile of v3, /device:TPU:1, one launch (start us, length us, event | category | flops | bytes accessed | tf_op | source)
XLA Modules:
  0.0 71.7 jit_solution(7987077982082223588)
XLA Ops:
  0.0 70.2 %shard_map.55 = bf16[128,256]{1,0:T(8,128)(2,1)} custom-call(s32[1,96]{1,0:T(1,128)} %bitcast.9, s32[1,96]{1,0:T(1,128)} %bitcast.10, s32[1,96]{1,0:T(1,128)} %bitcast.11, bf16[12,32,8,128]{3,2,1,0:T(8,128)(2,1)} %bitcast.7, bf16[16,64,256]{2,1,0:T(8,128)(2,1)} %bitcast.8), custom_call_target="tpu_custom_call" | custom-call | flops 301989888 | bytes 786432 | tf_op jit(solution)/shard_map/pallas_call | solution.py:332
  70.2 1.5 %copy.7 = bf16[128,256]{1,0:T(8,128)(2,1)} copy(bf16[128,256]{1,0:T(8,128)(2,1)} %shard_map.55) | data formatting | bytes 131072

commit v4 on v3

--- a/solution.py
+++ b/solution.py
@@ -13,6 +13,9 @@
 ROWS = B * B // LANES
 CAP = 3
 NX = 4
+PARTS = 1
+PIECE = B // PARTS
+TOGETHER = 4
 
 
 def shift(at, by, size):
@@ -31,8 +34,8 @@
     half, opposite = ny // 2, nz // 2
     places = n_row // 2
     row, split = lax.axis_index("row"), lax.axis_index("split")
-    x, z = row // nz, lax.rem(row, nz)
-    y, core = split // 2, lax.rem(split, 2)
+    x, z = lax.div(row, nz), lax.rem(row, nz)
+    y, core = lax.div(split, 2), lax.rem(split, 2)
     up_y, down_y = shift(y, 1, ny) * 2, shift(y, ny - 1, ny) * 2
     other = (row, y * 2 + 1 - core)
     above, above_other = (row, up_y + core), (row, up_y + 1 - core)
@@ -42,14 +45,14 @@
         return shift(x, dx, NX) * nz + shift(z, dz, nz)
 
     def place(q, x_of, z_of):
-        u = (places - q) % places
-        k = u // NX
-        odd = k % 2
-        px = (x_of + u % NX) % NX
-        dz = odd * ((k + 1) // 2) + (1 - odd) * (nz - k // 2)
-        flip = (k // (opposite - 1)) * (px % 2) if opposite > 1 else 0
+        u = lax.rem(places - q, places)
+        k = lax.div(u, NX)
+        odd = lax.rem(k, 2)
+        px = lax.rem(x_of + lax.rem(u, NX), NX)
+        dz = odd * lax.div(k + 1, 2) + (1 - odd) * (nz - lax.div(k, 2))
+        flip = lax.div(k, opposite - 1) * lax.rem(px, 2) if opposite > 1 else 0
         dz = dz + flip * (nz - 2 * dz)
-        return px, (z_of + dz) % nz
+        return px, lax.rem(z_of + dz, nz)
 
     def device(q):
         px, pz = place(q, x, z)
@@ -87,7 +90,7 @@
     px, pz = place(q_of, x, z)
     packed = jnp.zeros((places, LANES), jnp.int32)
     for i in range(2 * CAP):
-        to = px * nz + ((pz + opposite) % nz if i < CAP else pz)
+        to = px * nz + (lax.rem(pz + opposite, nz) if i < CAP else pz)
         hit = (to == dest) & (rank == i % CAP)
         which = jnp.sum(jnp.where(hit, t_of, 0), axis=1, keepdims=True)
         tag = jnp.sum(jnp.where(hit, label, 0), axis=1, keepdims=True)
@@ -142,10 +145,8 @@
             return carry
         return step
 
-    ahead_of_labels = min(9, places)
-    lax.fori_loop(1, ahead_of_labels, send_tiles(0), 0)
     lax.fori_loop(1, places, send_label, 0)
-    lax.fori_loop(ahead_of_labels, places, send_tiles(0), 0)
+    lax.fori_loop(1, places, send_tiles(0), 0)
     for part in range(2):
         blocks_to(recv, part, 0)
 
@@ -188,25 +189,30 @@
     fetch_plan.wait()
     fetches[4].wait()
 
-    def work(part, q):
-        products = []
-        for i in range(CAP):
-            block = recv[part, q, pl.ds(i * ROWS, ROWS), :]
-            lhs = jnp.concatenate([block[:, :B], block[:, B:]], axis=0)
-            col = plan_s[q, (2 + part) * CAP + i]
-            products.append(jnp.dot(lhs, dens_ref[col], preferred_element_type=jnp.float32))
-        for i in range(CAP):
-            sums[(part * places + q) * CAP + i] = products[i] + sums[plan_s[q, part * CAP + i]]
+    def work(part, q0):
+        for j in range(TOGETHER):
+            for i in range(CAP):
+                block = recv[part, q0 + j, pl.ds(i * ROWS, ROWS), :]
+                lhs = jnp.concatenate([block[:, :B], block[:, B:]], axis=0)
+                col = plan_s[q0 + j, (2 + part) * CAP + i]
+                sums[(part * places + q0 + j) * CAP + i] = jnp.dot(
+                    lhs, dens_ref[col], preferred_element_type=jnp.float32
+                )
+        for j in range(TOGETHER):
+            for i in range(CAP):
+                at = (part * places + q0 + j) * CAP + i
+                sums[at] = sums[at] + sums[plan_s[q0 + j, part * CAP + i]]
 
     def turns(part, start, stop):
-        def turn(q, carry):
-            tile_copy(part, q).wait_recv()
-            work(part, q)
-            if part == 0:
-                send_tiles(1)(q, 0)
+        def turn(n, carry):
+            for j in range(TOGETHER):
+                tile_copy(part, n * TOGETHER + j).wait_recv()
+            work(part, n * TOGETHER)
             return carry
 
         if start == 0:
+            for j in range(1, TOGETHER):
+                tile_copy(part, j).wait_recv()
             work(part, 0)
         lax.fori_loop(max(start, 1), stop, turn, 0)
 
@@ -239,21 +245,21 @@
         return remote(xsend.at[at], xrecv.at[at], x_ss.at[at], x_rs.at[at], other)
 
     def begin(part):
-        for c in range(2):
+        for c in range(2 if part == 0 else 0):
             shares = [partial(part, half, (core, 1 - core)[c], way) for way in range(2)]
-            for h in range(2):
+            for h in range(PARTS):
                 for way in range(2):
-                    first_send[part, way, c, h] = shares[way][h * ROWS:(h + 1) * ROWS]
+                    first_send[part, way, c, h] = shares[way][h * PIECE:(h + 1) * PIECE]
                     go(first(part, way, c, h))
-        for ahead in order:
+        for ahead in order if part == 0 else [half] + order:
             for b in range(2):
                 xsend[part, ahead, b] = partial(part, ahead, 1 - core, b)
             go(x_copy(part, ahead))
 
     def came(part, way, t, b, h):
-        if t == 0:
-            if way != b:
-                return 0.0
+        if t == 0 and way != b:
+            return 0.0
+        if t == 0 and part == 0:
             got = 0.0
             for c in range(2):
                 first(part, way, c, h).wait_recv()
@@ -262,6 +268,14 @@
         later(part, way, t, b, h).wait_recv()
         return later_recv[part, way, t, b, h]
 
+    def lead(part):
+        x_copy(part, half).wait_recv()
+        for way in range(2):
+            term = partial(part, half, core, way) + xrecv[part, half, way]
+            for h in range(PARTS):
+                later_send[part, way, 0, way, h] = term[h * PIECE:(h + 1) * PIECE]
+                go(later(part, way, 0, way, h))
+
     def forward(part, t):
         x_copy(part, half - t).wait_recv()
         x_copy(part, half + t).wait_recv()
@@ -269,30 +283,33 @@
             for way, b in ((0, 1 - step), (1, step)):
                 ahead = half - t if way == 0 else half + t
                 term = partial(part, ahead, core, b) + xrecv[part, ahead, b]
-                for h in range(2):
-                    later_send[part, way, t, b, h] = term[h * ROWS:(h + 1) * ROWS] + came(part, way, t - 1, b, h)
+                for h in range(PARTS):
+                    later_send[part, way, t, b, h] = term[h * PIECE:(h + 1) * PIECE] + came(part, way, t - 1, b, h)
                     go(later(part, way, t, b, h))
 
     def total(part, b, h):
         if b == 0 and h == 0:
             x_copy(part, 0).wait_recv()
         term = partial(part, 0, core, b) + xrecv[part, 0, b]
-        return term[h * ROWS:(h + 1) * ROWS] + came(part, 0, half - 1, b, h) + came(part, 1, half - 1, b, h)
+        return term[h * PIECE:(h + 1) * PIECE] + came(part, 0, half - 1, b, h) + came(part, 1, half - 1, b, h)
 
     def back(b, h):
         at = (b, h)
         return remote(back_send.at[at], back_recv.at[at], back_ss.at[at], back_rs.at[at], (at_row(0, opposite), split))
 
-    turns(0, 0, places)
+    groups = places // TOGETHER
+    lax.fori_loop(1, places, send_tiles(1), 0)
+    turns(0, 0, groups)
     begin(0)
-    cuts = [places * i // half for i in range(half + 1)]
-    for t in range(half):
-        if t > 0:
-            forward(0, t)
-        turns(1, cuts[t], cuts[t + 1])
+    for t in range(1, half - 1):
+        forward(0, t)
+    turns(1, 0, groups)
     begin(1)
+    if half > 1:
+        forward(0, half - 1)
+    lead(1)
     for b in range(2):
-        for h in range(2):
+        for h in range(PARTS):
             back_send[b, h] = total(0, b, h)
             go(back(b, h))
     for t in range(1, half):
@@ -310,7 +327,7 @@
     swap = (from_row == to_row % 2 * ROWS + to_row // 2).astype(jnp.bfloat16)
     for b in range(2):
         halves = []
-        for h in range(2):
+        for h in range(PARTS):
             whole = total(1, b, h)
             back(b, h).wait_recv()
             halves.append((whole + back_recv[b, h]).astype(jnp.bfloat16))
@@ -347,11 +364,11 @@
             smem((places + 8, LANES), i32),
             vmem((2 * places * CAP + 1, B, orbitals), f32),
             *[vmem((2, ny, 2, B, orbitals), f32)] * 2,
-            *[vmem((2, 2, 2, 2, ROWS, orbitals), f32)] * 2,
-            *[vmem((2, 2, half, 2, 2, ROWS, orbitals), f32)] * 2,
-            *[vmem((2, 2, ROWS, orbitals), f32)] * 2,
+            *[vmem((2, 2, 2, PARTS, PIECE, orbitals), f32)] * 2,
+            *[vmem((2, 2, half, 2, PARTS, PIECE, orbitals), f32)] * 2,
+            *[vmem((2, PARTS, PIECE, orbitals), f32)] * 2,
             dma((7,)), *[dma((places,))] * 2, *[dma((2, places))] * 2, *[dma((2, ny))] * 2,
-            *[dma((2, 2, 2, 2))] * 2, *[dma((2, 2, half, 2, 2))] * 2, *[dma((2, 2))] * 2,
+            *[dma((2, 2, 2, PARTS))] * 2, *[dma((2, 2, half, 2, PARTS))] * 2, *[dma((2, PARTS))] * 2,
         ],
         compiler_params=pltpu.CompilerParams(
             collective_id=0, has_side_effects=True, vmem_limit_bytes=63 * 2**20

time: 72.1 us -> 66.2 us (0.918)
  Pallas kernels: 70.2 us -> 64.3 us
    pallas_call x1, Pallas kernels: 70.2 us -> 64.3 us  [on_device(): pl.pallas_call(functools.partial(kernel, n_row, n_split), out_shape=jax.S...]
where the time goes in v4:
time: 66.2 us; the launch traced here: 65.7 us
  Pallas kernels  64.3 us (97%)
  local copies, waits for them, and re-layouts  1.47 us (2%)
    pallas_call x1, Pallas kernels, on_device(): pl.pallas_call(functools.partial(kernel, n_row, n_split), out_shape=jax.S...  64.3 us
    unnamed x1, local copies, waits for them, and re-layouts  1.47 us

profile of v4, /device:TPU:1, one launch (start us, length us, event | category | flops | bytes accessed | tf_op | source)
XLA Modules:
  0.0 65.7 jit_solution(4510611926340828618)
XLA Ops:
  0.0 64.3 %shard_map.55 = bf16[128,256]{1,0:T(8,128)(2,1)} custom-call(s32[1,96]{1,0:T(1,128)} %bitcast.9, s32[1,96]{1,0:T(1,128)} %bitcast.10, s32[1,96]{1,0:T(1,128)} %bitcast.11, bf16[12,32,8,128]{3,2,1,0:T(8,128)(2,1)} %bitcast.7, bf16[16,64,256]{2,1,0:T(8,128)(2,1)} %bitcast.8), custom_call_target="tpu_custom_call" | custom-call | flops 301989888 | bytes 786432 | tf_op jit(solution)/shard_map/pallas_call | solution.py:349
  64.3 1.5 %copy.7 = bf16[128,256]{1,0:T(8,128)(2,1)} copy(bf16[128,256]{1,0:T(8,128)(2,1)} %shard_map.55) | data formatting | bytes 131072

commit v5 on v4

--- a/solution.py
+++ b/solution.py
@@ -305,9 +305,9 @@
         forward(0, t)
     turns(1, 0, groups)
     begin(1)
+    lead(1)
     if half > 1:
         forward(0, half - 1)
-    lead(1)
     for b in range(2):
         for h in range(PARTS):
             back_send[b, h] = total(0, b, h)

time: 66.2 us -> 67.9 us (1.026)
  the two profiles are of different devices: /device:TPU:1 before, /device:TPU:16 now
where the time goes in v5:
time: 67.9 us; the launch traced here: 67.7 us
  Pallas kernels  66.3 us (98%)
  local copies, waits for them, and re-layouts  1.47 us (2%)
    pallas_call x1, Pallas kernels, on_device(): pl.pallas_call(functools.partial(kernel, n_row, n_split), out_shape=jax.S...  66.3 us
    unnamed x1, local copies, waits for them, and re-layouts  1.47 us

profile of v5, /device:TPU:16, one launch (start us, length us, event | category | flops | bytes accessed | tf_op | source)
XLA Modules:
  0.0 67.7 jit_solution(11383772169446861927)
XLA Ops:
  0.0 66.3 %shard_map.55 = bf16[128,256]{1,0:T(8,128)(2,1)} custom-call(s32[1,96]{1,0:T(1,128)} %bitcast.9, s32[1,96]{1,0:T(1,128)} %bitcast.10, s32[1,96]{1,0:T(1,128)} %bitcast.11, bf16[12,32,8,128]{3,2,1,0:T(8,128)(2,1)} %bitcast.7, bf16[16,64,256]{2,1,0:T(8,128)(2,1)} %bitcast.8), custom_call_target="tpu_custom_call" | custom-call | flops 301989888 | bytes 786432 | tf_op jit(solution)/shard_map/pallas_call | solution.py:349
  66.3 1.5 %copy.7 = bf16[128,256]{1,0:T(8,128)(2,1)} copy(bf16[128,256]{1,0:T(8,128)(2,1)} %shard_map.55) | data formatting | bytes 131072
